TPU v7x, 512 devices: a whole 4x4x16 slice. The times are simulated.
512 devices in a mesh: row: 16 (over y, x_hi, core), col: 32 (over z, x_lo).
Axes of the slice: x: 4 (x_hi: 2, x_lo: 2; x = x_hi * 2 + x_lo), y: 4, z: 16, core: 2. Of those that a mesh axis runs over, the one named last changes fastest.
Arguments:
- hess_inv: float32 [16384, 16384], P('row', 'col'), as said below
- weights: bfloat16 [6144, 16384], P('row', 'col'), may hold values from -6 to 6
- removed: int32 [512], replicated, may hold values from 0 to 16383, as said below
Outputs:
- hess_out: float32 [16384, 16384], P('row', 'col')
- weight_out: bfloat16 [6144, 16384], P('row', 'col')
Inputs may be any that keep to these rules, and one draw needn't show every extreme that they name: `removed`: sorted ascending and distinct; each aligned block of 512 columns holds at most 48 of them, and at least one block holds exactly 48. `hess_inv`: symmetric and positive definite.
All inputs are finite; a program needn't handle non-finite values.
Results may differ from a plain program's by a relative error of at most 0.005.
Values may be sent and summed in bfloat16 or wider, within the bound.
A program may use at most 64 MiB of HBM per device.

v0:
```python
import jax
import jax.numpy as jnp
from jax import lax
from jax.sharding import PartitionSpec as P

MOST = 48


def spread(block, axis, owner):
    block = jnp.where(lax.axis_index(axis) == owner, block, jnp.zeros_like(block))
    return lax.psum(block, axis)


def pick_owned(source, removed, tile_index, tile_size, slot_count, which_axis):
    before = jnp.sum((removed < tile_index * tile_size).astype(jnp.int32))
    within = jnp.sum((removed // tile_size == tile_index).astype(jnp.int32))
    slot_rank = jnp.arange(slot_count, dtype=jnp.int32)
    chosen = jnp.clip(before + slot_rank, 0, removed.shape[0] - 1)
    local_col = jnp.clip(removed[chosen] - tile_index * tile_size, 0, tile_size - 1)
    taken_part = jnp.take(source, local_col, axis=which_axis)
    live_slot = slot_rank < within
    mask_shape = [1, 1]
    mask_shape[which_axis] = slot_count
    return jnp.where(live_slot.reshape(mask_shape), taken_part, jnp.zeros((), taken_part.dtype))


def slot_map(removed, tile_size, slot_count):
    which_tile = removed // tile_size
    first_pos = jnp.sum(
        (removed[None, :] < (which_tile * tile_size)[:, None]).astype(jnp.int32), axis=1
    )
    position = jnp.arange(removed.shape[0], dtype=jnp.int32)
    return which_tile * slot_count + position - first_pos


def on_device(hess_inv, weights, removed):
    row_count = lax.axis_size("row")
    col_count = lax.axis_size("col")
    col_index = lax.axis_index("col")
    row_tile, col_tile = hess_inv.shape
    tile_ratio = col_count // row_count
    col_slots = slot_map(removed, col_tile, MOST)
    packed_weight = pick_owned(weights, removed, col_index, col_tile, MOST, 1)
    packed_hess = pick_owned(hess_inv, removed, col_index, col_tile, MOST, 1)
    wide_hess, weight_wide = (
        lax.all_gather(packed_hess, "col", axis=1, tiled=True),
        lax.all_gather(packed_weight.astype(jnp.float32), "col", axis=1, tiled=True).astype(
            packed_weight.dtype
        ),
    )
    left_side = jnp.take(wide_hess, col_slots, axis=1)
    weight_left = jnp.take(weight_wide, col_slots, axis=1)
    mirror_part = lax.dynamic_slice_in_dim(
        left_side, col_index % tile_ratio * col_tile, col_tile, 0
    )
    mirrored = spread(mirror_part, "row", col_index // tile_ratio)
    upper_rows = mirrored.T
    own_cols = pick_owned(upper_rows, removed, col_index, col_tile, MOST, 1)
    block_wide = lax.all_gather(own_cols, "col", axis=1, tiled=True)
    removed_block = jnp.take(block_wide, col_slots, axis=1)
    factor = jnp.linalg.cholesky(removed_block)
    identity = jnp.eye(removed_block.shape[0], dtype=jnp.float32)
    factor_inv = jax.scipy.linalg.solve_triangular(factor, identity, lower=True)
    block_inv = jnp.dot(factor_inv.T, factor_inv, precision=lax.Precision.HIGHEST)
    coupling = jnp.dot(block_inv, upper_rows, precision=lax.Precision.HIGHEST)
    correction = jnp.dot(left_side, coupling, precision=lax.Precision.HIGHEST)
    hess_out = hess_inv - correction
    weight_fix = jnp.dot(weight_left.astype(jnp.float32), coupling, precision=lax.Precision.HIGHEST)
    weight_out = (weights.astype(jnp.float32) - weight_fix).astype(jnp.bfloat16)
    return (hess_out, weight_out)


def solution(mesh):
    placed = (P("row", "col"), P("row", "col"), P())
    return jax.shard_map(
        on_device,
        mesh=mesh,
        in_specs=placed,
        out_specs=(P("row", "col"), P("row", "col")),
        check_vma=False,
    )
```

profile of v0, /device:TPU:8, one launch (start us, length us, event | category | flops | bytes accessed | tf_op | source)
XLA Modules:
  0.0 811.1 jit_solution(553122249612259826)
XLA Ops:
  7.2 1.9 copy.13
  14.4 161.7 %all-gather.4.cloned.1.call-done = f32[1024,1536]{0,1:T(8,128)} async-done(((f32[1024,48]{0,1:T(8,128)}), f32[1024,1536]{0,1:T(8,128)}) %all-gather.4.cloned.1.call-update) | async-done | bytes 6291472 | tf_op jit(solution)/shard_map/all_gather | solution.py:46
  176.1 6.4 gather_fusion.2
  187.2 144.6 %all-reduce.3.cloned.1.call-done = f32[512,512]{0,1:T(8,128)} async-done(((f32[512,512]{0,1:T(8,128)}), f32[512,512]{0,1:T(8,128)}) %all-reduce.3.cloned.1.call-update) | async-done | bytes 1048592 | tf_op jit(solution)/shard_map/psum | solution.py:11
  337.1 136.0 %all-gather.8.cloned.1.call-done = bf16[384,1536]{0,1:T(8,128)(2,1)} async-done(((bf16[384,48]{0,1:T(8,128)(2,1)}), bf16[384,1536]{0,1:T(8,128)(2,1)}) %all-gather.8.cloned.1.call-update) | async-done | bytes 1179664 | tf_op jit(solution)/shard_map/all_gather | solution.py:47
  473.2 3.2 gather_fusion.6
  476.4 135.1 %all-gather.6.cloned.1.call-done = f32[512,1536]{0,1:T(8,128)} async-done(((f32[512,48]{0,1:T(8,128)}), f32[512,1536]{0,1:T(8,128)}) %all-gather.6.cloned.1.call-update) | async-done | bytes 3145744 | tf_op jit(solution)/shard_map/all_gather | solution.py:59
  611.6 4.4 gather_fusion.4
  617.1 2.5 copy.15
  622.0 11.7 %cholesky.102 = f32[128,128]{1,0:T(8,128)S(1)} custom-call(f32[128,128]{1,0:T(8,128)S(1)} %cholesky.260), custom_call_target="Cholesky" | custom-call | tf_op jit(solution)/shard_map/jit(cholesky)/cholesky | solution.py:61
  635.9 11.3 %custom-call.31 = f32[1,128,128]{1,2,0:T(8,128)} custom-call(f32[1,128,128]{2,1,0:T(8,128)} %get-tuple-element.33), custom_call_target="InvertDiagBlocksLowerTriangular" | custom-call | tf_op jit(solution)/shard_map/jit(cholesky)/cholesky | solution.py:61
  651.0 13.2 %cholesky.213 = f32[128,128]{1,0:T(8,128)} custom-call(f32[128,128]{1,0:T(8,128)} %cholesky.264), custom_call_target="Cholesky" | custom-call | tf_op jit(solution)/shard_map/jit(cholesky)/cholesky | solution.py:61
  665.7 11.4 %custom-call.32 = f32[1,128,128]{1,2,0:T(8,128)} custom-call(f32[1,128,128]{2,1,0:T(8,128)} %get-tuple-element.30), custom_call_target="InvertDiagBlocksLowerTriangular" | custom-call | tf_op jit(solution)/shard_map/jit(cholesky)/cholesky | solution.py:61
  680.8 13.2 %cholesky.234 = f32[128,128]{1,0:T(8,128)} custom-call(f32[128,128]{1,0:T(8,128)} %cholesky.269), custom_call_target="Cholesky" | custom-call | tf_op jit(solution)/shard_map/jit(cholesky)/cholesky | solution.py:61
  695.5 11.3 %custom-call.33 = f32[1,128,128]{1,2,0:T(8,128)} custom-call(f32[1,128,128]{2,1,0:T(8,128)} %get-tuple-element.27), custom_call_target="InvertDiagBlocksLowerTriangular" | custom-call | tf_op jit(solution)/shard_map/jit(cholesky)/cholesky | solution.py:61
  709.7 13.2 %cholesky.251 = f32[128,128]{1,0:T(8,128)} custom-call(f32[128,128]{1,0:T(8,128)} %convolution_subtract_fusion.7), custom_call_target="Cholesky" | custom-call | tf_op jit(solution)/shard_map/jit(cholesky)/cholesky | solution.py:61
  731.0 14.4 %while.1 = (s32[]{:T(128)}, f32[512,512]{1,0:T(8,128)}, s32[4,2]{0,1:T(2,128)S(1)}, f32[4,128,128]{2,1,0:T(8,128)}, s32[]{:T(128)}) while((s32[]{:T(128)}, f32[512,512]{1,0:T(8,128)}, s32[4,2]{0,1:T(2,128)S(1)}, f32[4,128,128]{2,1,0:T(8,128)}, s32[]{:T(128)}) %tuple.34), condition=%wide.while_cond, body=%wide.while_body.sunk | while | flops 2 | bytes 132205 | solution.py:63
  731.7 2.9 bitcast_dynamic-update-slice_fusion.2
  735.3 2.9 bitcast_dynamic-update-slice_fusion.2
  738.9 2.9 bitcast_dynamic-update-slice_fusion.2
  742.5 2.9 bitcast_dynamic-update-slice_fusion.2
  745.4 40.7 %custom-call.34 = f32[4,128,128]{1,2,0:T(8,128)} custom-call(f32[4,128,128]{2,1,0:T(8,128)} %get-tuple-element.9), custom_call_target="InvertDiagBlocksLowerTriangular" | custom-call | tf_op jit(solution)/shard_map/jit(_solve_triangular)/triangular_solve | solution.py:63
  793.9 1.9 fusion.1
  797.7 4.8 convolution_subtract_fusion
  (94 shorter events, 53.7 us)
Async XLA Ops:
  7.2 169.0 %all-gather.4.cloned.1.call-start = ((), (), s32[]{:S(2)}) async-start(), calls=%async_computation | async-start | bytes 6488064 | tf_op jit(solution)/shard_map/all_gather | solution.py:46
  7.2 2.0 copy-start
  14.0 317.7 %all-reduce.3.cloned.1.call-start = ((), (), s32[]{:S(2)}) async-start(), calls=%async_computation.1 | async-start | bytes 2097152 | tf_op jit(solution)/shard_map/psum | solution.py:11
  184.3 1.2 copy-start.5
  185.4 287.7 %all-gather.8.cloned.1.call-start = ((), (), s32[]{:S(2)}) async-start(), calls=%async_computation.3 | async-start | bytes 1216512 | tf_op jit(solution)/shard_map/all_gather | solution.py:47
  187.1 424.4 %all-gather.6.cloned.1.call-start = ((), (), s32[]{:S(2)}) async-start(), calls=%async_computation.2 | async-start | bytes 3244032 | tf_op jit(solution)/shard_map/all_gather | solution.py:59
  621.0 1.0 copy-start.4
  633.7 0.6 copy-start.10
  649.7 0.7 copy-start.7
  679.5 0.6 copy-start.8
  730.3 59.7 %copy-start.3 = (f32[512,512]{1,0:T(8,128)S(1)}, f32[512,512]{1,0:T(8,128)}, u32[]{:S(2)}) copy-start(f32[512,512]{1,0:T(8,128)} %fusion.19) | copy-start | bytes 3145732
  786.1 5.2 copy-start.9
  791.8 4.0 copy-start.2
  795.8 1.9 copy-start.1
  797.7 4.8 copy-start.6
Sparse Core Ops, SparseCore 0:
  14.2 161.9 all-gather.3
  185.6 146.1 all-reduce.2
  334.1 139.0 all-gather.7
  475.9 135.6 all-gather.5
where the time goes:
time: 817 us; the launch traced here: 811 us
  waiting for transfers between devices  578 us (71%)
  other arithmetic  147 us (18%)
  local copies, waits for them, and re-layouts  43.2 us (5%)
  matrix products  25.9 us (3%)
  between operations  17 us (2%)
    all_gather x1, waiting for transfers between devices, on_device(): lax.all_gather(packed_hess, 'col', axis=1, tiled=True)  162 us
    psum x1, waiting for transfers between devices, spread(): return lax.psum(block, axis)  145 us
    all_gather x1, waiting for transfers between devices, on_device(): lax.all_gather(packed_weight.astype(jnp.float32), 'col', axis=1, tiled=True)  136 us
    all_gather x1, waiting for transfers between devices, on_device(): block_wide = lax.all_gather(own_cols, 'col', axis=1, tiled=True)  135 us
    another operation x15, other arithmetic, on_device(): factor = jnp.linalg.cholesky(removed_block)  92.5 us
    another operation x3, other arithmetic, on_device(): factor_inv = jax.scipy.linalg.solve_triangular(factor, identity, lower=True)  42.4 us
  transfers between devices with their start and end apart: 4, of which 4 were waited for; matrix products, arithmetic and copies ran while one was open for 1% of the time, Pallas kernels for 0%

commit v1 on v0

--- a/solution.py
+++ b/solution.py
@@ -44,9 +44,12 @@
     packed_hess = pick_owned(hess_inv, removed, col_index, col_tile, MOST, 1)
     wide_hess, weight_wide = (
         lax.all_gather(packed_hess, "col", axis=1, tiled=True),
-        lax.all_gather(packed_weight.astype(jnp.float32), "col", axis=1, tiled=True).astype(
-            packed_weight.dtype
-        ),
+        jnp.concatenate(
+            lax.all_to_all(
+                jnp.stack([packed_weight.astype(jnp.float32)] * lax.axis_size("col")), "col", 0, 0
+            ),
+            axis=1,
+        ).astype(packed_weight.dtype),
     )
     left_side = jnp.take(wide_hess, col_slots, axis=1)
     weight_left = jnp.take(weight_wide, col_slots, axis=1)

time: 817 us -> 682 us (0.83)
  the two profiles are of different devices: /device:TPU:8 before, /device:TPU:64 now
where the time goes in v1:
time: 682 us; the launch traced here: 677 us
  waiting for transfers between devices  452 us (66%)
  other arithmetic  132 us (19%)
  local copies, waits for them, and re-layouts  39.7 us (6%)
  matrix products  22.6 us (3%)
  between operations  16.9 us (2%)
  starting transfers between devices  13 us (2%)
    all_gather x1, waiting for transfers between devices, on_device(): lax.all_gather(packed_hess, 'col', axis=1, tiled=True)  159 us
    psum x1, waiting for transfers between devices, spread(): return lax.psum(block, axis)  155 us
    another operation x15, other arithmetic, on_device(): factor = jnp.linalg.cholesky(removed_block)  79.2 us
    all_gather x1, waiting for transfers between devices, on_device(): block_wide = lax.all_gather(own_cols, 'col', axis=1, tiled=True)  78.1 us
    all_to_all x1, waiting for transfers between devices, on_device(): lax.all_to_all(jnp.stack([packed_weight.astype(jnp.float32)] * lax.axis_s...  60.4 us
    another operation x3, other arithmetic, on_device(): factor_inv = jax.scipy.linalg.solve_triangular(factor, identity, lower=True)  41.4 us
    another operation x12, local copies, waits for them, and re-layouts  14.1 us
  transfers between devices with their start and end apart: 4, of which 4 were waited for; matrix products, arithmetic and copies ran while one was open for 1% of the time, Pallas kernels for 0%

profile of v1, /device:TPU:64, one launch (start us, length us, event | category | flops | bytes accessed | tf_op | source)
XLA Modules:
  0.0 676.7 jit_solution(16475931207156814844)
XLA Ops:
  7.2 1.9 copy.13
  14.4 159.0 %all-gather.3.cloned.1.call-done = f32[1024,1536]{0,1:T(8,128)} async-done(((f32[1024,48]{0,1:T(8,128)}), f32[1024,1536]{0,1:T(8,128)}) %all-gather.3.cloned.1.call-update) | async-done | bytes 6291472 | tf_op jit(solution)/shard_map/all_gather | solution.py:46
  173.4 6.4 gather_fusion.2
  182.7 154.6 %all-reduce.3.cloned.1.call-done = f32[512,512]{0,1:T(8,128)} async-done(((f32[512,512]{0,1:T(8,128)}), f32[512,512]{0,1:T(8,128)}) %all-reduce.3.cloned.1.call-update) | async-done | bytes 1048592 | tf_op jit(solution)/shard_map/psum | solution.py:11
  343.4 12.9 %all-to-all-start = ((bf16[32,384,48]{1,2,0:T(8,128)(2,1)}), bf16[32,384,48]{1,2,0:T(8,128)(2,1)S(1)}, u32[]{:S(2)}, u32[]{:S(2)}) async-start(bf16[32,384,48]{1,2,0:T(8,128)(2,1)} %stack.2), calls=%async_computation | async-start | bytes 2359296 | tf_op jit(solution)/shard_map/all_to_all | solution.py:48
  358.2 60.4 %all-to-all-done = bf16[32,384,48]{1,2,0:T(8,128)(2,1)S(1)} async-done(((bf16[32,384,48]{1,2,0:T(8,128)(2,1)}), bf16[32,384,48]{1,2,0:T(8,128)(2,1)S(1)}, u32[]{:S(2)}, u32[]{:S(2)}) %all-to-all-start) | async-done | bytes 1179680 | tf_op jit(solution)/shard_map/all_to_all | solution.py:48
  418.5 2.6 gather_fusion.6
  421.1 78.1 %all-gather.5.cloned.1.call-done = f32[512,1536]{0,1:T(8,128)} async-done(((f32[512,48]{0,1:T(8,128)}), f32[512,1536]{0,1:T(8,128)}) %all-gather.5.cloned.1.call-update) | async-done | bytes 3145744 | tf_op jit(solution)/shard_map/all_gather | solution.py:62
  499.2 4.4 gather_fusion.4
  504.7 2.5 copy.15
  509.7 11.7 %cholesky.102 = f32[128,128]{1,0:T(8,128)S(1)} custom-call(f32[128,128]{1,0:T(8,128)S(1)} %cholesky.260), custom_call_target="Cholesky" | custom-call | tf_op jit(solution)/shard_map/jit(cholesky)/cholesky | solution.py:64
  521.6 9.8 %custom-call.31 = f32[1,128,128]{1,2,0:T(8,128)S(1)} custom-call(f32[1,128,128]{2,1,0:T(8,128)S(1)} %get-tuple-element.33), custom_call_target="InvertDiagBlocksLowerTriangular" | custom-call | tf_op jit(solution)/shard_map/jit(cholesky)/cholesky | solution.py:64
  533.9 11.7 %cholesky.213 = f32[128,128]{1,0:T(8,128)S(1)} custom-call(f32[128,128]{1,0:T(8,128)S(1)} %cholesky.264), custom_call_target="Cholesky" | custom-call | tf_op jit(solution)/shard_map/jit(cholesky)/cholesky | solution.py:64
  545.7 10.0 %custom-call.32 = f32[1,128,128]{1,2,0:T(8,128)S(1)} custom-call(f32[1,128,128]{2,1,0:T(8,128)S(1)} %get-tuple-element.30), custom_call_target="InvertDiagBlocksLowerTriangular" | custom-call | tf_op jit(solution)/shard_map/jit(cholesky)/cholesky | solution.py:64
  557.2 11.7 %cholesky.234 = f32[128,128]{1,0:T(8,128)S(1)} custom-call(f32[128,128]{1,0:T(8,128)S(1)} %cholesky.269), custom_call_target="Cholesky" | custom-call | tf_op jit(solution)/shard_map/jit(cholesky)/cholesky | solution.py:64
  568.9 9.8 %custom-call.33 = f32[1,128,128]{1,2,0:T(8,128)S(1)} custom-call(f32[1,128,128]{2,1,0:T(8,128)S(1)} %get-tuple-element.27), custom_call_target="InvertDiagBlocksLowerTriangular" | custom-call | tf_op jit(solution)/shard_map/jit(cholesky)/cholesky | solution.py:64
  580.2 11.7 %cholesky.251 = f32[128,128]{1,0:T(8,128)S(1)} custom-call(f32[128,128]{1,0:T(8,128)S(1)} %convolution_subtract_fusion.7), custom_call_target="Cholesky" | custom-call | tf_op jit(solution)/shard_map/jit(cholesky)/cholesky | solution.py:64
  598.4 14.1 %while.1 = (s32[]{:T(128)}, f32[512,512]{1,0:T(8,128)}, s32[4,2]{0,1:T(2,128)S(1)}, f32[4,128,128]{2,1,0:T(8,128)}, s32[]{:T(128)}) while((s32[]{:T(128)}, f32[512,512]{1,0:T(8,128)}, s32[4,2]{0,1:T(2,128)S(1)}, f32[4,128,128]{2,1,0:T(8,128)}, s32[]{:T(128)}) %tuple.34), condition=%wide.while_cond, body=%wide.while_body.sunk | while | flops 2 | bytes 132205 | solution.py:66
  599.1 2.9 bitcast_dynamic-update-slice_fusion.2
  602.7 2.9 bitcast_dynamic-update-slice_fusion.2
  606.2 2.9 bitcast_dynamic-update-slice_fusion.2
  609.7 2.8 bitcast_dynamic-update-slice_fusion.2
  612.6 40.1 %custom-call.34 = f32[4,128,128]{1,2,0:T(8,128)S(1)} custom-call(f32[4,128,128]{2,1,0:T(8,128)} %get-tuple-element.9), custom_call_target="InvertDiagBlocksLowerTriangular" | custom-call | tf_op jit(solution)/shard_map/jit(_solve_triangular)/triangular_solve | solution.py:66
  663.3 4.8 convolution_subtract_fusion
  (86 shorter events, 44.2 us)
Async XLA Ops:
  7.2 166.2 %all-gather.3.cloned.1.call-start = ((), (), s32[]{:S(2)}) async-start(), calls=%async_computation.1 | async-start | bytes 6488064 | tf_op jit(solution)/shard_map/all_gather | solution.py:46
  7.2 2.0 copy-start
  14.0 323.3 %all-reduce.3.cloned.1.call-start = ((), (), s32[]{:S(2)}) async-start(), calls=%async_computation.2 | async-start | bytes 2097152 | tf_op jit(solution)/shard_map/psum | solution.py:11
  182.7 316.6 %all-gather.5.cloned.1.call-start = ((), (), s32[]{:S(2)}) async-start(), calls=%async_computation.3 | async-start | bytes 3244032 | tf_op jit(solution)/shard_map/all_gather | solution.py:62
  343.4 75.2 %all-to-all-start = ((bf16[32,384,48]{1,2,0:T(8,128)(2,1)}), bf16[32,384,48]{1,2,0:T(8,128)(2,1)S(1)}, u32[]{:S(2)}, u32[]{:S(2)}) async-start(bf16[32,384,48]{1,2,0:T(8,128)(2,1)} %stack.2), calls=%async_computation | async-start | bytes 2359296 | tf_op jit(solution)/shard_map/all_to_all | solution.py:48
  508.7 1.0 copy-start.4
  598.4 57.1 %copy-start.3 = (f32[512,512]{1,0:T(8,128)S(1)}, f32[512,512]{1,0:T(8,128)}, u32[]{:S(2)}) copy-start(f32[512,512]{1,0:T(8,128)} %fusion.19) | copy-start | bytes 3145732
  657.3 4.0 copy-start.2
  661.4 1.9 copy-start.1
  663.3 4.9 copy-start.5
  663.3 4.9 copy-start.6
Sparse Core Ops, SparseCore 0:
  14.2 159.1 all-gather.2
  182.8 154.4 all-reduce.2
  340.4 158.8 all-gather.4

commit v2 on v0

--- a/solution.py
+++ b/solution.py
@@ -8,7 +8,7 @@
 
 def spread(block, axis, owner):
     block = jnp.where(lax.axis_index(axis) == owner, block, jnp.zeros_like(block))
-    return lax.psum(block, axis)
+    return jnp.sum(lax.all_gather(block, axis), axis=0)
 
 
 def pick_owned(source, removed, tile_index, tile_size, slot_count, which_axis):

time: 817 us -> 791 us (0.968)
  waiting for transfers between devices: 578 us -> 512 us
  local copies, waits for them, and re-layouts: 43.2 us -> 65.4 us
  other arithmetic: 147 us -> 163 us
    psum x1 -> x0, waiting for transfers between devices: 145 us -> none  [spread(): return lax.psum(block, axis)]
    all_gather x0 -> x1, waiting for transfers between devices: none -> 118 us  [spread(): return jnp.sum(lax.all_gather(block, axis), axis=0)]
    all_gather x1, waiting for transfers between devices: 136 us -> 97.7 us  [on_device(): lax.all_gather(packed_weight.astype(jnp.float32), 'col', axis=1, tiled=True)]
    unnamed x24 -> x19, local copies, waits for them, and re-layouts: 5.04 us -> 24.5 us
    reduce_sum x0 -> x1, other arithmetic: none -> 9.82 us  [spread(): return jnp.sum(lax.all_gather(block, axis), axis=0)]
  transfers between devices with their start and end apart: 4 -> 4, of which waited for: 4 -> 4; matrix products, arithmetic and copies ran while one was open for 1% -> 5% of each run, Pallas kernels for 0% -> 0%
where the time goes in v2:
time: 791 us; the launch traced here: 786 us
  waiting for transfers between devices  512 us (65%)
  other arithmetic  163 us (21%)
  local copies, waits for them, and re-layouts  65.4 us (8%)
  matrix products  28.4 us (4%)
  between operations  16.8 us (2%)
    all_gather x1, waiting for transfers between devices, on_device(): lax.all_gather(packed_hess, 'col', axis=1, tiled=True)  162 us
    all_gather x1, waiting for transfers between devices, on_device(): block_wide = lax.all_gather(own_cols, 'col', axis=1, tiled=True)  135 us
    all_gather x1, waiting for transfers between devices, spread(): return jnp.sum(lax.all_gather(block, axis), axis=0)  118 us
    all_gather x1, waiting for transfers between devices, on_device(): lax.all_gather(packed_weight.astype(jnp.float32), 'col', axis=1, tiled=True)  97.7 us
    another operation x15, other arithmetic, on_device(): factor = jnp.linalg.cholesky(removed_block)  95.6 us
    another operation x3, other arithmetic, on_device(): factor_inv = jax.scipy.linalg.solve_triangular(factor, identity, lower=True)  43.1 us
    unnamed x19, local copies, waits for them, and re-layouts  24.5 us
  transfers between devices with their start and end apart: 4, of which 4 were waited for; matrix products, arithmetic and copies ran while one was open for 5% of the time, Pallas kernels for 0%

profile of v2, /device:TPU:8, one launch (start us, length us, event | category | flops | bytes accessed | tf_op | source)
XLA Modules:
  0.0 786.1 jit_solution(4570730467513687484)
XLA Ops:
  15.8 161.7 %all-gather.6.cloned.1.call-done = f32[1024,1536]{0,1:T(8,128)} async-done(((f32[1024,48]{0,1:T(8,128)}), f32[1024,1536]{0,1:T(8,128)}) %all-gather.6.cloned.1.call-update) | async-done | bytes 6291472 | tf_op jit(solution)/shard_map/all_gather | solution.py:46
  177.5 6.4 gather_fusion.2
  188.7 117.6 %all-gather.12.cloned.1.call-done = f32[8192,512]{0,1:T(8,128)} async-done(((f32[512,512]{0,1:T(8,128)}), f32[8192,512]{0,1:T(8,128)}) %all-gather.12.cloned.1.call-update) | async-done | bytes 16777232 | tf_op jit(solution)/shard_map/all_gather | solution.py:11
  306.3 20.0 %copy.19 = f32[64,8,16,512]{3,2,1,0:T(8,128)} copy(f32[64,8,16,512]{3,1,2,0:T(8,128)} %bitcast.71) | data formatting | bytes 33554432
  326.3 9.8 %bitcast_reduce_fusion = f32[512,512]{0,1:T(8,128)S(1)} fusion(f32[64,8,16,512]{3,2,1,0:T(8,128)} %copy.19), kind=kLoop, calls=%fused_computation.9 | loop fusion | flops 3932160 | bytes 17825792 | tf_op jit(solution)/shard_map/reduce_sum | solution.py:11
  342.0 97.7 %all-gather.10.cloned.1.call-done = bf16[384,1536]{0,1:T(8,128)(2,1)} async-done(((bf16[384,48]{0,1:T(8,128)(2,1)}), bf16[384,1536]{0,1:T(8,128)(2,1)}) %all-gather.10.cloned.1.call-update) | async-done | bytes 1179664 | tf_op jit(solution)/shard_map/all_gather | solution.py:47
  439.6 3.2 gather_fusion.6
  442.9 135.0 %all-gather.8.cloned.1.call-done = f32[512,1536]{0,1:T(8,128)} async-done(((f32[512,48]{0,1:T(8,128)}), f32[512,1536]{0,1:T(8,128)}) %all-gather.8.cloned.1.call-update) | async-done | bytes 3145744 | tf_op jit(solution)/shard_map/all_gather | solution.py:59
  577.8 4.8 gather_fusion.4
  585.0 2.6 copy.17
  591.0 13.2 %cholesky.102 = f32[128,128]{1,0:T(8,128)} custom-call(f32[128,128]{1,0:T(8,128)} %cholesky.260), custom_call_target="Cholesky" | custom-call | tf_op jit(solution)/shard_map/jit(cholesky)/cholesky | solution.py:61
  607.5 11.3 %custom-call.31 = f32[1,128,128]{1,2,0:T(8,128)} custom-call(f32[1,128,128]{2,1,0:T(8,128)} %get-tuple-element.33), custom_call_target="InvertDiagBlocksLowerTriangular" | custom-call | tf_op jit(solution)/shard_map/jit(cholesky)/cholesky | solution.py:61
  623.3 13.2 %cholesky.213 = f32[128,128]{1,0:T(8,128)} custom-call(f32[128,128]{1,0:T(8,128)} %cholesky.264), custom_call_target="Cholesky" | custom-call | tf_op jit(solution)/shard_map/jit(cholesky)/cholesky | solution.py:61
  639.3 11.7 %custom-call.32 = f32[1,128,128]{1,2,0:T(8,128)} custom-call(f32[1,128,128]{2,1,0:T(8,128)} %get-tuple-element.30), custom_call_target="InvertDiagBlocksLowerTriangular" | custom-call | tf_op jit(solution)/shard_map/jit(cholesky)/cholesky | solution.py:61
  655.5 13.2 %cholesky.234 = f32[128,128]{1,0:T(8,128)} custom-call(f32[128,128]{1,0:T(8,128)} %cholesky.269), custom_call_target="Cholesky" | custom-call | tf_op jit(solution)/shard_map/jit(cholesky)/cholesky | solution.py:61
  670.9 11.3 %custom-call.33 = f32[1,128,128]{1,2,0:T(8,128)} custom-call(f32[1,128,128]{2,1,0:T(8,128)} %get-tuple-element.27), custom_call_target="InvertDiagBlocksLowerTriangular" | custom-call | tf_op jit(solution)/shard_map/jit(cholesky)/cholesky | solution.py:61
  685.9 13.2 %cholesky.251 = f32[128,128]{1,0:T(8,128)} custom-call(f32[128,128]{1,0:T(8,128)} %convolution_subtract_fusion.7), custom_call_target="Cholesky" | custom-call | tf_op jit(solution)/shard_map/jit(cholesky)/cholesky | solution.py:61
  706.2 14.1 %while.1 = (s32[]{:T(128)}, f32[512,512]{1,0:T(8,128)}, s32[4,2]{0,1:T(2,128)S(1)}, f32[4,128,128]{2,1,0:T(8,128)}, s32[]{:T(128)}) while((s32[]{:T(128)}, f32[512,512]{1,0:T(8,128)}, s32[4,2]{0,1:T(2,128)S(1)}, f32[4,128,128]{2,1,0:T(8,128)}, s32[]{:T(128)}) %tuple.34), condition=%wide.while_cond, body=%wide.while_body.sunk | while | flops 2 | bytes 132705 | solution.py:63
  706.9 2.9 bitcast_dynamic-update-slice_fusion.2
  710.4 2.9 bitcast_dynamic-update-slice_fusion.2
  714.0 2.9 bitcast_dynamic-update-slice_fusion.2
  717.5 2.8 bitcast_dynamic-update-slice_fusion.2
  720.3 40.7 %custom-call.34 = f32[4,128,128]{1,2,0:T(8,128)} custom-call(f32[4,128,128]{2,1,0:T(8,128)} %get-tuple-element.9), custom_call_target="InvertDiagBlocksLowerTriangular" | custom-call | tf_op jit(solution)/shard_map/jit(_solve_triangular)/triangular_solve | solution.py:63
  772.7 4.8 convolution_subtract_fusion
  (90 shorter events, 66.6 us)
Async XLA Ops:
  7.2 170.3 %all-gather.6.cloned.1.call-start = ((), (), s32[]{:S(2)}) async-start(), calls=%async_computation | async-start | bytes 6488064 | tf_op jit(solution)/shard_map/all_gather | solution.py:46
  13.9 1.5 copy-start
  15.4 290.9 %all-gather.12.cloned.1.call-start = ((), (), s32[]{:S(2)}) async-start(), calls=%async_computation.3 | async-start | bytes 17825792 | tf_op jit(solution)/shard_map/all_gather | solution.py:11
  185.7 1.2 copy-start.3
  186.8 252.8 %all-gather.10.cloned.1.call-start = ((), (), s32[]{:S(2)}) async-start(), calls=%async_computation.2 | async-start | bytes 1216512 | tf_op jit(solution)/shard_map/all_gather | solution.py:47
  188.5 389.4 %all-gather.8.cloned.1.call-start = ((), (), s32[]{:S(2)}) async-start(), calls=%async_computation.1 | async-start | bytes 3244032 | tf_op jit(solution)/shard_map/all_gather | solution.py:59
  589.3 1.0 copy-start.2
  622.0 0.7 copy-start.5
  654.3 0.6 copy-start.6
  761.0 5.3 copy-start.7
  770.8 1.9 copy-start.1
  772.7 4.8 copy-start.4
Sparse Core Ops, SparseCore 0:
  15.5 161.9 all-gather.5
  186.9 119.3 all-gather.11
  308.4 131.1 all-gather.9
  442.2 135.6 all-gather.7
